TPU v7x, 512 devices: a whole 4x4x16 slice. The times are simulated.
512 devices in a mesh: row: 32 (over z, y_hi), col: 16 (over x, y_lo, core).
Axes of the slice: x: 4, y: 4 (y_hi: 2, y_lo: 2; y = y_hi * 2 + y_lo), z: 16, core: 2. Of those that a mesh axis runs over, the one named last changes fastest.
Arguments:
- factor_band: float32 [4096, 131072], P('row', 'col'), may hold values from -0.015625 to 0.015625
- normals: float32 [131072, 384], P('col', 'row'), may hold values from -6 to 6
- site_mean: float32 [4096], P('row'), may hold values from 5 to 10
- site_spread: float32 [4096], P('row'), may hold values from 1 to 4
- site_capacity: float32 [4096], P('row'), may hold values from 0.1 to 1
- site_kind: int32 [4096], P('row'), may hold values 0 or 1
- site_plant: int32 [4096], P('row'), may hold values from 0 to 2047
Outputs:
- plant_output: float32 [384, 2048], P('col', 'row')
All inputs are finite; a program needn't handle non-finite values. No bound on the sum of `site_kind` on one device may be relied on, other than what follows from the above.
Results may differ from a plain program's by a relative error of at most 0.000096.
Values sent between devices are 32-bit elements; how exact they have to be, the bound alone decides.
A program may use at most 128 MiB of HBM per device.

v0:
```python
import jax
import jax.numpy as jnp
from jax import lax
from jax.sharding import PartitionSpec as P

PLANTS = 2048


def body(factor_band, normals, site_mean, site_spread, site_capacity, site_kind, site_plant):
    share = normals.shape[1] * lax.axis_size("row") // lax.axis_size("col")
    partial_rows = lax.dot_general(
        lax.all_gather(normals, "row", axis=1, tiled=True),
        factor_band,
        (((0,), (1,)), ((), ())),
        precision=lax.Precision.HIGHEST,
        preferred_element_type=jnp.float32,
    )
    total = lax.psum(partial_rows, "col")
    samples = lax.dynamic_slice_in_dim(total, lax.axis_index("col") * share, share, 0)
    speed = site_mean[None, :] + site_spread[None, :] * samples
    positive = jnp.maximum(speed, 0.0)
    wind = jnp.clip((positive * positive * positive - 27.0) / (1728.0 - 27.0), 0.0, 1.0)
    solar = jnp.clip(speed / 12.0, 0.0, 1.0)
    power = jnp.where(site_kind[None, :] == 1, solar, wind) * site_capacity[None, :]
    onehot = (site_plant[:, None] == jnp.arange(PLANTS, dtype=jnp.int32)[None, :]).astype(
        jnp.float32
    )
    terms = jnp.dot(
        power, onehot, precision=lax.Precision.HIGHEST, preferred_element_type=jnp.float32
    )
    return lax.psum_scatter(terms, "row", scatter_dimension=1, tiled=True)


def solution(mesh):
    in_specs = (P("row", "col"), P("col", "row"), P("row"), P("row"), P("row"), P("row"), P("row"))
    out_specs = P("col", "row")
    return jax.shard_map(body, mesh=mesh, in_specs=in_specs, out_specs=out_specs, check_vma=False)
```

profile of v0, /device:TPU:1, one launch (start us, length us, event | category | flops | bytes accessed | tf_op | source)
XLA Modules:
  0.0 1094.7 jit_solution(14875359424413770468)
XLA Ops:
  6.5 0.0 all-gather.3.cloned.1.call-start
  6.5 0.7 all-gather.3.cloned.1.call-update
  7.3 0.0 all-reduce.2.cloned.1.call-start
  7.3 275.8 %all-gather.3.cloned.1.call-done = f32[32,12,8192]{2,1,0:T(8,128)} async-done(((f32[1,12,8192]{2,1,0:T(8,128)}), f32[32,12,8192]{2,1,0:T(8,128)}) %all-gather.3.cloned.1.call-update) | async-done | bytes 12582928 | tf_op jit(solution)/shard_map/all_gather | solution.py:12
  283.1 12.5 %reshape.7 = f32[384,8192]{1,0:T(8,128)} reshape(f32[32,12,8192]{2,1,0:T(8,128)} %all-gather.3.cloned.1.call-done) | data formatting | bytes 25165824
  295.6 0.0 copy-start.4
  295.6 0.0 copy-start
  295.6 0.0 copy-start.1
  295.6 0.0 copy-start.2
  295.7 0.0 copy-start.3
  295.7 14.2 %fusion.28 = f32[384,128]{1,0:T(8,128)} fusion(f32[384,8192]{1,0:T(8,128)} %reshape.7, f32[128,8192]{1,0:T(8,128)} %param.7), kind=kOutput, calls=%fused_computation.31 | convolution fusion | flops 4831838208 | bytes 16973824 | tf_op jit(solution)/shard_map/dot_general | solution.py:11
  309.9 0.0 all-reduce.2.cloned.1.call-update
  309.9 0.0 reduce-scatter.4.cloned.1.call-start
  310.0 0.0 copy-done.4
  310.0 123.2 %all-reduce.2.cloned.1.call-done = f32[384,128]{1,0:T(8,128)} async-done(((f32[384,128]{1,0:T(8,128)}), f32[384,128]{1,0:T(8,128)}) %all-reduce.2.cloned.1.call-update) | async-done | bytes 196624 | tf_op jit(solution)/shard_map/psum | solution.py:18
  433.2 0.0 copy-done
  433.2 0.0 copy-done.1
  433.2 0.0 copy-done.2
  433.2 0.0 copy-done.3
  433.2 2.7 convolution_bitcast_fusion
  435.9 0.0 reduce-scatter.4.cloned.1.call-update
  435.9 650.8 %reduce-scatter.4.cloned.1.call-done = f32[64,24]{1,0:T(8,128)} async-done(((f32[2048,24]{1,0:T(8,128)}), f32[64,24]{1,0:T(8,128)}) %reduce-scatter.4.cloned.1.call-update) | async-done | bytes 6160
  1086.7 1.4 copy.9
  (1 shorter events, 0.0 us)
Async XLA Ops:
  6.5 276.6 %all-gather.3.cloned.1.call-start = ((), (), s32[]{:S(2)}) async-start(), calls=%async_computation.2 | async-start | bytes 17301504 | tf_op jit(solution)/shard_map/all_gather | solution.py:12
  7.3 425.9 %all-reduce.2.cloned.1.call-start = ((), (), s32[]{:S(2)}) async-start(), calls=%async_computation.1 | async-start | bytes 393216 | tf_op jit(solution)/shard_map/psum | solution.py:18
  295.6 14.3 %copy-start.4 = (s32[128]{0:T(128)S(1)}, s32[128]{0:T(128)}, u32[]{:S(2)}) copy-start(s32[128]{0:T(128)} %param.12) | copy-start | bytes 1540
  295.6 137.5 %copy-start = (s32[128]{0:T(128)S(1)}, s32[128]{0:T(128)}, u32[]{:S(2)}) copy-start(s32[128]{0:T(128)} %param.13) | copy-start | bytes 1540
  295.6 137.5 %copy-start.1 = (f32[128]{0:T(128)S(1)}, f32[128]{0:T(128)}, u32[]{:S(2)}) copy-start(f32[128]{0:T(128)} %param.11) | copy-start | bytes 1540
  295.6 137.5 %copy-start.2 = (f32[128]{0:T(128)S(1)}, f32[128]{0:T(128)}, u32[]{:S(2)}) copy-start(f32[128]{0:T(128)} %param.10) | copy-start | bytes 1540
  295.7 137.5 %copy-start.3 = (f32[128]{0:T(128)S(1)}, f32[128]{0:T(128)}, u32[]{:S(2)}) copy-start(f32[128]{0:T(128)} %param.9) | copy-start | bytes 1540
  309.9 776.8 %reduce-scatter.4.cloned.1.call-start = ((), (), s32[]{:S(2)}) async-start(), calls=%async_computation.3 | async-start | bytes 1081344
Sparse Core Ops, SparseCore 0:
  10.5 272.6 all-gather.2
  310.0 123.0 all-reduce.1
  438.2 648.4 reduce-scatter.3
where the time goes:
time: 1110 us; the launch traced here: 1090 us
  waiting for transfers between devices  1050 us (95%)
  matrix products  17 us (2%)
  local copies, waits for them, and re-layouts  13.9 us (1%)
  between operations  13.1 us (1%)
    unnamed x4, waiting for transfers between devices  652 us
    all_gather x1, waiting for transfers between devices, body(): lax.all_gather(normals, 'row', axis=1, tiled=True)  276 us
    psum x1, waiting for transfers between devices, body(): total = lax.psum(partial_rows, 'col')  123 us
  transfers between devices with their start and end apart: 3, of which 3 were waited for; matrix products, arithmetic and copies ran while one was open for 0% of the time, Pallas kernels for 0%

commit v1 on v0

v1 whole, which is shorter than its diff:
```python
import functools

import jax
import jax.numpy as jnp
from jax import lax
from jax.experimental import pallas as pl
from jax.experimental.pallas import tpu as pltpu
from jax.sharding import PartitionSpec as P

MESH = pl.DeviceIdType.MESH
LAG = 1


def split_bf16(v):
    hi = v.astype(jnp.bfloat16)
    return hi, (v - hi.astype(jnp.float32)).astype(jnp.bfloat16)


def nt_dot(a, b):
    return lax.dot_general(a, b, (((1,), (1,)), ((), ())), preferred_element_type=jnp.float32)


def kernel(
    nz, nc, kh, plants,
    f_ref, n_ref, mean_ref, spread_ref, cap_ref, kind_ref, plant_ref, out_ref,
    nown, nbuf, bsend, brecv, fown, frecv, fh, fl, par, onehot, acc, rsend, rrecv, zsend, zrecv,
    loc_sem, nx_send, nx_recv, fx_send, fx_recv, ring_send, ring_recv, r_send, r_recv, z_send, z_recv,
):
    half = nz // 2
    zero = half - 1
    near = half - 2
    peers = 2 * nc
    rows = 2 * nz
    row, col = lax.axis_index("row"), lax.axis_index("col")
    z, yh = row // 2, lax.rem(row, 2)
    partner = row + 1 - 2 * yh
    right = lax.rem(z + 1, nz) * 2 + yh
    left = lax.rem(z + nz - 1, nz) * 2 + yh
    mine = pl.multiple_of(yh * kh, kh)
    other = pl.multiple_of((1 - yh) * kh, kh)
    ua, up = 2 * yh, 2 - 2 * yh

    load_a = pltpu.make_async_copy(n_ref.at[pl.ds(0, 8), pl.ds(mine, kh)], nbuf.at[zero, ua], loc_sem.at[0])
    load_n = pltpu.make_async_copy(n_ref, nown, loc_sem.at[1])
    load_f = pltpu.make_async_copy(f_ref.at[:, pl.ds(mine, kh)], fown, loc_sem.at[2])
    load_a.start()
    load_n.start()
    load_f.start()

    barrier = pltpu.get_barrier_semaphore()

    @pl.loop(0, peers)
    def _(i):
        r, c = z * 2 + i // nc, lax.rem(i, nc)

        @pl.when(jnp.logical_or(r != row, c != col))
        def _():
            pl.semaphore_signal(barrier, inc=1, device_id=(r, c), device_id_type=MESH)

    @pl.loop(0, rows)
    def _(r):
        @pl.when(r != row)
        def _():
            pl.semaphore_signal(barrier, inc=1, device_id=(r, col), device_id_type=MESH)

    row_of = lax.broadcasted_iota(jnp.int32, (8, 128), 0)
    packed = jnp.zeros((8, 128), jnp.float32)
    for i, ref in enumerate((mean_ref, spread_ref, cap_ref, kind_ref, plant_ref)):
        packed = jnp.where(row_of == i, ref[...].astype(jnp.float32).reshape(1, 128), packed)
    par[yh] = packed
    load_n.wait()
    q = kh // 2
    bsend[0:4, :] = nown[8:12, pl.ds(other, q)]
    bsend[4:8, :] = nown[8:12, pl.ds(pl.multiple_of(other + q, q), q)]
    load_a.wait()

    pl.semaphore_wait(barrier, peers - 1 + rows - 1)

    def to_partner(src, dst, i):
        return pltpu.make_async_remote_copy(
            src, dst, nx_send.at[i], nx_recv.at[i], device_id=(partner, col), device_id_type=MESH
        )

    def ring(s, h, way):
        unit = (ua, up, 1)[s]
        slot = zero - h if way == 0 else zero + h
        to = slot - 1 if way == 0 else slot + 1
        if h < half - 1:
            src, dst = nbuf.at[slot, unit], nbuf.at[to, unit]
        else:
            to = nz - 1
            part = pl.ds(0, q) if way == 0 else pl.ds(q, q)
            src, dst = nbuf.at[slot, unit, :, part], nbuf.at[to, unit, :, part]
        i = (s * half + h) * 2 + way
        return pltpu.make_async_remote_copy(
            src, dst, ring_send.at[i], ring_recv.at[i],
            device_id=(right if way == 0 else left, col), device_id_type=MESH,
        )

    swap_a = to_partner(n_ref.at[pl.ds(0, 8), pl.ds(other, kh)], nbuf.at[zero, ua], 0)
    swap_b = to_partner(bsend, brecv, 1)
    swap_p = to_partner(par.at[yh], par.at[yh], 2)
    ring(0, 0, 0).start()
    ring(0, 0, 1).start()
    swap_a.start()
    swap_b.start()
    swap_p.start()
    swap_f = [
        pltpu.make_async_remote_copy(
            f_ref.at[pl.ds(i * 32, 32), pl.ds(other, kh)], frecv.at[pl.ds(i * 32, 32)],
            fx_send.at[i], fx_recv.at[i], device_id=(partner, col), device_id_type=MESH,
        )
        for i in range(4)
    ]
    for c in swap_f:
        c.start()

    sites = f_ref.shape[0]

    def split_f(src, base, i):
        @pl.loop(0, 4)
        def _(j):
            hi, lo = split_bf16(src[pl.ds(pl.multiple_of(i * 32, 32), 32), pl.ds(pl.multiple_of(j * (kh // 4), kh // 4), kh // 4)])
            at = pl.ds(pl.multiple_of(base + i * 32, 32), 32)
            cols = pl.ds(pl.multiple_of(j * (kh // 4), kh // 4), kh // 4)
            fh[at, cols] = hi
            fl[at, cols] = lo

    def build_t1():
        swap_b.wait_recv()
        for j in range(2):
            own = nown[8:12, pl.ds(pl.multiple_of(mine + j * q, q), q)]
            got = brecv[4 * j : 4 * j + 4, :]
            both = jnp.concatenate([own, got], axis=0)
            flip = jnp.concatenate([got, own], axis=0)
            nbuf[zero, 1, :, j * q : (j + 1) * q] = jnp.where(yh == 0, both, flip)

    def build_onehot():
        ids = jnp.concatenate([par[0], par[1]], axis=1)[4:5, :]
        ids = jnp.broadcast_to(ids, (128, 2 * sites))
        ids = ids.T

        @pl.loop(0, plants // 128)
        def _(j):
            lane = lax.broadcasted_iota(jnp.int32, (2 * sites, 128), 1) + j * 128
            onehot[j] = jnp.where(ids == lane.astype(jnp.float32), 1.0, 0.0).astype(jnp.bfloat16)

    def matmul(slots, k_from, k_to, first):
        step = kh // 4
        m = 24 * len(slots)

        @pl.loop(k_from, k_to)
        def _(k):
            cols = pl.ds(pl.multiple_of(k * step, step), step)
            x = jnp.concatenate([nbuf[s, :, :, cols].reshape(24, step) for s in slots], axis=0)
            hi, lo = split_bf16(x)
            a, b = fh[:, cols], fl[:, cols]
            t = nt_dot(hi, a) + nt_dot(lo, a) + nt_dot(hi, b)

            @pl.when(k == 0)
            def _():
                acc[0:m, :] = t

            @pl.when(k != 0)
            def _():
                acc[0:m, :] += t

    def send_partials(slots):
        me = yh * nc + col
        for i, s in enumerate(slots):
            block = lax.rem(z + s - zero + nz, nz)
            t1 = acc[24 * i + 8 : 24 * i + 16, :]
            for y in range(2):
                a = acc[24 * i + 16 * y : 24 * i + 16 * y + 8, :]
                b = t1[4 * y : 4 * y + 4, :]
                b = jnp.concatenate([b[:, 0:128], b[:, 128:256]], axis=0)
                msg = jnp.concatenate([a, b], axis=1)
                self_ = jnp.logical_and(block == col, yh == y)

                @pl.when(self_)
                def _():
                    rrecv[me] = msg

                @pl.when(jnp.logical_not(self_))
                def _():
                    rsend[2 * s + y] = msg
                    pltpu.make_async_remote_copy(
                        rsend.at[2 * s + y], rrecv.at[me], r_send, r_recv,
                        device_id=(z * 2 + y, block), device_id_type=MESH,
                    ).start()

    def finish_sites():
        pltpu.make_async_copy(rrecv.at[pl.ds(0, peers - 1)], rrecv.at[pl.ds(0, peers - 1)], r_recv).wait()
        tot = rrecv[0]
        for i in range(1, peers):
            tot = tot + rrecv[i]
        b = jnp.concatenate([tot[0:4, 256:384], tot[4:8, 256:384]], axis=1)
        samples = jnp.concatenate([tot[:, 0:256], b, b], axis=0)
        p = jnp.concatenate([par[0], par[1]], axis=1)
        speed = p[0:1] + p[1:2] * samples
        positive = jnp.maximum(speed, 0.0)
        wind = jnp.clip((positive * positive * positive - 27.0) / (1728.0 - 27.0), 0.0, 1.0)
        solar = jnp.clip(speed / 12.0, 0.0, 1.0)
        power = jnp.where(p[3:4] == 1.0, solar, wind) * p[2:3]
        p0, rest = power.astype(jnp.bfloat16), power
        rest = rest - p0.astype(jnp.float32)
        p1 = rest.astype(jnp.bfloat16)
        p2 = (rest - p1.astype(jnp.float32)).astype(jnp.bfloat16)
        pieces = jnp.concatenate([p0, p1, p2], axis=0)
        low = lax.broadcasted_iota(jnp.int32, (8, 128), 1) < 64

        for j in range(nz):
            t = jnp.dot(pieces, onehot[j], preferred_element_type=jnp.float32)
            t = t[0:16] + t[16:32] + t[32:48]
            a, c = t[0:8], t[8:16]
            msgs = jnp.where(low, a, pltpu.roll(c, 64, 1)), jnp.where(low, pltpu.roll(a, 64, 1), c)
            for y in range(2):
                zsend[2 * j + y] = msgs[y]

        @pl.loop(0, rows)
        def _(r):
            @pl.when(r == row)
            def _():
                zrecv[row] = zsend[r]

            @pl.when(r != row)
            def _():
                pltpu.make_async_remote_copy(
                    zsend.at[r], zrecv.at[row], z_send, z_recv, device_id=(r, col), device_id_type=MESH
                ).start()

    slots_a = list(range(zero - near, zero + near + 1))
    slots_b = [s for s in range(nz) if s not in slots_a]
    off = lax.rem(col - z + zero + nz, nz)
    is_a = jnp.logical_and(off >= slots_a[0], off <= slots_a[-1])

    def forward(s, h):
        if h >= 1:
            for way in range(2):
                ring(s, h - 1, way).wait_recv()
                ring(s, h, way).start()
        elif s:
            if s == 1:
                swap_a.wait_recv()
            else:
                build_t1()
            ring(s, 0, 0).start()
            ring(s, 0, 1).start()

    for t in range(1, half + LAG):
        for s in range(3):
            h = t if s == 0 else t - LAG
            if h < half:
                forward(s, h)
        if t == 1:
            load_f.wait()
        if 1 <= t <= 2:
            for i in range(2):
                split_f(fown, yh * sites, 2 * t - 2 + i)
        if t == 2:
            swap_p.wait_recv()
            build_onehot()
        if 3 <= t <= 6 and half == 8:
            swap_f[t - 3].wait_recv()
            split_f(frecv, (1 - yh) * sites, t - 3)
        if half != 8 and t == 1:
            for i in range(4):
                swap_f[i].wait_recv()
                split_f(frecv, (1 - yh) * sites, i)

    matmul(slots_a, 0, 4, True)
    send_partials(slots_a)

    @pl.when(is_a)
    def _():
        finish_sites()

    for s in range(3):
        for way in range(2):
            ring(s, half - 1, way).wait_recv()
    matmul(slots_b, 0, 4, True)
    send_partials(slots_b)

    @pl.when(jnp.logical_not(is_a))
    def _():
        finish_sites()

    swap_a.wait_send()
    swap_b.wait_send()
    swap_p.wait_send()
    for c in swap_f:
        c.wait_send()
    for s in range(3):
        for h in range(half):
            for way in range(2):
                ring(s, h, way).wait_send()
    pltpu.make_async_copy(rsend.at[pl.ds(0, peers - 1)], rsend.at[pl.ds(0, peers - 1)], r_send).wait()
    pltpu.make_async_copy(zsend.at[pl.ds(0, rows - 1)], zsend.at[pl.ds(0, rows - 1)], z_send).wait()
    pltpu.make_async_copy(zrecv.at[pl.ds(0, rows - 1)], zrecv.at[pl.ds(0, rows - 1)], z_recv).wait()
    s0, s1 = zrecv[0], zrecv[1]
    for i in range(1, nz):
        s0 = s0 + zrecv[2 * i]
        s1 = s1 + zrecv[2 * i + 1]
    out_ref[0:8, :] = s0[:, 0:64]
    out_ref[8:12, :] = s0[0:4, 64:128]
    out_ref[12:20, :] = s1[:, 0:64]
    out_ref[20:24, :] = s1[0:4, 64:128]


def body(factor_band, normals, site_mean, site_spread, site_capacity, site_kind, site_plant):
    rows, nc = lax.axis_size("row"), lax.axis_size("col")
    nz = rows // 2
    half = nz // 2
    sites, k = factor_band.shape
    kh = k // 2
    plants = 64 * rows
    f32, bf16 = jnp.float32, jnp.bfloat16
    vmem = pl.BlockSpec(memory_space=pltpu.VMEM)
    hbm = pl.BlockSpec(memory_space=pl.ANY)
    dma = pltpu.SemaphoreType.DMA
    return pl.pallas_call(
        functools.partial(kernel, nz, nc, kh, plants),
        out_shape=jax.ShapeDtypeStruct((24, 64), f32),
        in_specs=[hbm, hbm] + [vmem] * 5,
        out_specs=vmem,
        scratch_shapes=[
            pltpu.VMEM((12, k), f32),
            pltpu.VMEM((nz, 3, 8, kh), f32),
            pltpu.VMEM((8, kh // 2), f32),
            pltpu.VMEM((8, kh // 2), f32),
            pltpu.VMEM((sites, kh), f32),
            pltpu.VMEM((sites, kh), f32),
            pltpu.VMEM((2 * sites, kh), bf16),
            pltpu.VMEM((2 * sites, kh), bf16),
            pltpu.VMEM((2, 8, 128), f32),
            pltpu.VMEM((nz, 2 * sites, 128), bf16),
            pltpu.VMEM((24 * (nz - 3), 2 * sites), f32),
            pltpu.VMEM((2 * nc, 8, 384), f32),
            pltpu.VMEM((2 * nc, 8, 384), f32),
            pltpu.VMEM((rows, 8, 128), f32),
            pltpu.VMEM((rows, 8, 128), f32),
            dma((3,)), dma((3,)), dma((3,)), dma((4,)), dma((4,)),
            dma((6 * half,)), dma((6 * half,)),
            dma, dma, dma, dma,
        ],
        compiler_params=pltpu.CompilerParams(
            collective_id=0, has_side_effects=True, vmem_limit_bytes=48 * 1024 * 1024
        ),
        cost_estimate=pl.CostEstimate(flops=3 * 2 * 24 * nz * 2 * sites * kh, bytes_accessed=4 * sites * k, transcendentals=0),
        name="band_to_plants",
    )(factor_band, normals.T, site_mean, site_spread, site_capacity, site_kind, site_plant)


def solution(mesh):
    in_specs = (P("row", "col"), P("col", "row"), P("row"), P("row"), P("row"), P("row"), P("row"))
    return jax.shard_map(body, mesh=mesh, in_specs=in_specs, out_specs=P("col", "row"), check_vma=False)
```

time: 1110 us -> 119 us (0.11); the launches traced: 1090 us -> 119 us
  waiting for transfers between devices: 1050 us -> 0 us
  Pallas kernels: 0 us -> 112 us
  matrix products: 17 us -> 0 us
  between operations: 13.1 us -> 0.02 us
    unnamed x4 -> x0, waiting for transfers between devices: 652 us -> none
    all_gather x1 -> x0, waiting for transfers between devices: 276 us -> none  [body(): lax.all_gather(normals, 'row', axis=1, tiled=True)]
    psum x1 -> x0, waiting for transfers between devices: 123 us -> none  [body(): total = lax.psum(partial_rows, 'col')]
    pallas_call x0 -> x1, Pallas kernels: none -> 112 us  [body(): pl.pallas_call(functools.partial(kernel, nz, nc, kh, plants), out_shape=j...]
    dot_general x1 -> x0, matrix products: 14.2 us -> none  [body(): lax.dot_general(lax.all_gather(normals, 'row', axis=1, tiled=True), facto...]
  transfers between devices with their start and end apart: 3 -> 0, of which waited for: 3 -> 0; matrix products, arithmetic and copies ran while one was open for 0% -> 0% of each run, Pallas kernels for 0% -> 0%
where the time goes in v1:
time: 119 us
  Pallas kernels  112 us (94%)
  local copies, waits for them, and re-layouts  7.1 us (6%)
    pallas_call x1, Pallas kernels, body(): pl.pallas_call(functools.partial(kernel, nz, nc, kh, plants), out_shape=j...  112 us
    unnamed x15, local copies, waits for them, and re-layouts  7.1 us

profile of v1, /device:TPU:1, one launch (start us, length us, event | category | flops | bytes accessed | tf_op | source)
XLA Modules:
  0.0 118.7 jit_solution(4941992570857926583)
XLA Ops:
  0.0 0.0 copy-start
  0.0 2.2 %copy-done = f32[128,8192]{1,0:T(8,128)S(1)} copy-done((f32[128,8192]{1,0:T(8,128)S(1)}, f32[128,8192]{1,0:T(8,128)}, u32[]{:S(2)}) %copy-start) | copy-done | bytes 4194328
  2.2 0.0 copy-start.1
  2.2 1.0 copy-done.1
  3.2 0.0 copy-start.2
  3.2 0.7 copy-done.2
  3.9 0.0 copy-start.3
  3.9 0.7 copy-done.3
  4.5 0.0 copy-start.4
  4.5 0.7 copy-done.4
  5.2 0.0 copy-start.5
  5.2 0.7 copy-done.5
  5.9 0.0 copy-start.6
  5.9 0.7 copy-done.6
  6.5 111.6 %band_to_plants.1 = f32[24,64]{1,0:T(8,128)S(1)} custom-call(f32[128,8192]{1,0:T(8,128)S(1)} %copy-done, f32[12,8192]{1,0:T(8,128)S(1)} %bitcast.1, f32[128]{0:T(128)S(1)} %copy-done.2, f32[128]{0:T(128)S(1)} %copy-done.3, f32[128]{0:T(128)S(1)} %copy-done.4, s32[128]{0:T(128)S(1)} %copy-done.5, s32[128]{0:T(128)S(1)} %copy-done.6), custom_call_target="tpu_custom_call" | custom-call | flops 2415919104 | bytes 4194304 | tf_op jit(solution)/shard_map/band_to_plants/pallas_call | solution.py:321
  118.1 0.6 copy.9
Async XLA Ops:
  0.0 2.2 %copy-start = (f32[128,8192]{1,0:T(8,128)S(1)}, f32[128,8192]{1,0:T(8,128)}, u32[]{:S(2)}) copy-start(f32[128,8192]{1,0:T(8,128)} %f_ref.1) | copy-start | bytes 12582916
  2.2 1.0 copy-start.1
  3.2 0.7 copy-start.2
  3.9 0.7 copy-start.3
  4.5 0.7 copy-start.4
  5.2 0.7 copy-start.5
  5.9 0.7 copy-start.6

commit v2 on v1

--- a/solution.py
+++ b/solution.py
@@ -8,7 +8,6 @@
 from jax.sharding import PartitionSpec as P
 
 MESH = pl.DeviceIdType.MESH
-LAG = 1
 
 
 def split_bf16(v):
@@ -23,7 +22,7 @@
 def kernel(
     nz, nc, kh, plants,
     f_ref, n_ref, mean_ref, spread_ref, cap_ref, kind_ref, plant_ref, out_ref,
-    nown, nbuf, bsend, brecv, fown, frecv, fh, fl, par, onehot, acc, rsend, rrecv, zsend, zrecv,
+    sitef, sitei, nown, nbuf, bsend, brecv, fown, frecv, fh, fl, par, onehot, acc, rsend, rrecv, zsend, zrecv,
     loc_sem, nx_send, nx_recv, fx_send, fx_recv, ring_send, ring_recv, r_send, r_recv, z_send, z_recv,
 ):
     half = nz // 2
@@ -40,33 +39,37 @@
     other = pl.multiple_of((1 - yh) * kh, kh)
     ua, up = 2 * yh, 2 - 2 * yh
 
+    barrier = pltpu.get_barrier_semaphore()
+    for r in (right, left):
+        pl.semaphore_signal(barrier, inc=1, device_id=(r, col), device_id_type=MESH)
+
+    @pl.loop(0, peers)
+    def _(i):
+        r, c = z * 2 + i // nc, lax.rem(i, nc)
+
+        @pl.when(jnp.logical_or(r != row, c != col))
+        def _():
+            pl.semaphore_signal(barrier, inc=1, device_id=(r, c), device_id_type=MESH)
+
     load_a = pltpu.make_async_copy(n_ref.at[pl.ds(0, 8), pl.ds(mine, kh)], nbuf.at[zero, ua], loc_sem.at[0])
     load_n = pltpu.make_async_copy(n_ref, nown, loc_sem.at[1])
     load_f = pltpu.make_async_copy(f_ref.at[:, pl.ds(mine, kh)], fown, loc_sem.at[2])
+    floats, ints = (mean_ref, spread_ref, cap_ref), (kind_ref, plant_ref)
+    load_s = [pltpu.make_async_copy(r, sitef.at[i], loc_sem.at[3 + i]) for i, r in enumerate(floats)]
+    load_s += [pltpu.make_async_copy(r, sitei.at[i], loc_sem.at[6 + i]) for i, r in enumerate(ints)]
+    load_n.start()
     load_a.start()
-    load_n.start()
+    for c in load_s:
+        c.start()
     load_f.start()
-
-    barrier = pltpu.get_barrier_semaphore()
-
-    @pl.loop(0, peers)
-    def _(i):
-        r, c = z * 2 + i // nc, lax.rem(i, nc)
-
-        @pl.when(jnp.logical_or(r != row, c != col))
-        def _():
-            pl.semaphore_signal(barrier, inc=1, device_id=(r, c), device_id_type=MESH)
-
-    @pl.loop(0, rows)
-    def _(r):
-        @pl.when(r != row)
-        def _():
-            pl.semaphore_signal(barrier, inc=1, device_id=(r, col), device_id_type=MESH)
 
     row_of = lax.broadcasted_iota(jnp.int32, (8, 128), 0)
     packed = jnp.zeros((8, 128), jnp.float32)
-    for i, ref in enumerate((mean_ref, spread_ref, cap_ref, kind_ref, plant_ref)):
-        packed = jnp.where(row_of == i, ref[...].astype(jnp.float32).reshape(1, 128), packed)
+    for c in load_s:
+        c.wait()
+    for i in range(5):
+        v = sitef[i : i + 1, :] if i < 3 else sitei[i - 3 : i - 2, :].astype(jnp.float32)
+        packed = jnp.where(row_of == i, v, packed)
     par[yh] = packed
     load_n.wait()
     q = kh // 2
@@ -74,7 +77,7 @@
     bsend[4:8, :] = nown[8:12, pl.ds(pl.multiple_of(other + q, q), q)]
     load_a.wait()
 
-    pl.semaphore_wait(barrier, peers - 1 + rows - 1)
+    pl.semaphore_wait(barrier, peers - 1 + 2)
 
     def to_partner(src, dst, i):
         return pltpu.make_async_remote_copy(
@@ -143,19 +146,20 @@
         @pl.loop(0, plants // 128)
         def _(j):
             lane = lax.broadcasted_iota(jnp.int32, (2 * sites, 128), 1) + j * 128
-            onehot[j] = jnp.where(ids == lane.astype(jnp.float32), 1.0, 0.0).astype(jnp.bfloat16)
-
-    def matmul(slots, k_from, k_to, first):
-        step = kh // 4
+            onehot[:, pl.ds(pl.multiple_of(j * 128, 128), 128)] = jnp.where(ids == lane.astype(jnp.float32), 1.0, 0.0).astype(jnp.bfloat16)
+
+    def matmul(slots, parts, k_from, k_to):
+        step = kh // parts
         m = 24 * len(slots)
 
         @pl.loop(k_from, k_to)
         def _(k):
             cols = pl.ds(pl.multiple_of(k * step, step), step)
             x = jnp.concatenate([nbuf[s, :, :, cols].reshape(24, step) for s in slots], axis=0)
-            hi, lo = split_bf16(x)
-            a, b = fh[:, cols], fl[:, cols]
-            t = nt_dot(hi, a) + nt_dot(lo, a) + nt_dot(hi, b)
+            hi = x.astype(jnp.bfloat16).astype(jnp.float32)
+            hl = jnp.concatenate([hi, x - hi], axis=0).astype(jnp.bfloat16)
+            t = nt_dot(hl, fh[:, cols])
+            t = t[0:m] + t[m : 2 * m] + nt_dot(hl[0:m], fl[:, cols])
 
             @pl.when(k == 0)
             def _():
@@ -165,9 +169,9 @@
             def _():
                 acc[0:m, :] += t
 
-    def send_partials(slots):
+    def send_partials(slots, first=0):
         me = yh * nc + col
-        for i, s in enumerate(slots):
+        for i, s in enumerate(slots, first):
             block = lax.rem(z + s - zero + nz, nz)
             t1 = acc[24 * i + 8 : 24 * i + 16, :]
             for y in range(2):
@@ -209,37 +213,34 @@
         pieces = jnp.concatenate([p0, p1, p2], axis=0)
         low = lax.broadcasted_iota(jnp.int32, (8, 128), 1) < 64
 
+        sums = jnp.dot(pieces, onehot[...], preferred_element_type=jnp.float32)
+        sums = sums[0:16] + sums[16:32] + sums[32:48]
         for j in range(nz):
-            t = jnp.dot(pieces, onehot[j], preferred_element_type=jnp.float32)
-            t = t[0:16] + t[16:32] + t[32:48]
-            a, c = t[0:8], t[8:16]
+            a, c = sums[0:8, 128 * j : 128 * (j + 1)], sums[8:16, 128 * j : 128 * (j + 1)]
             msgs = jnp.where(low, a, pltpu.roll(c, 64, 1)), jnp.where(low, pltpu.roll(a, 64, 1), c)
             for y in range(2):
                 zsend[2 * j + y] = msgs[y]
 
-        @pl.loop(0, rows)
-        def _(r):
-            @pl.when(r == row)
-            def _():
-                zrecv[row] = zsend[r]
-
-            @pl.when(r != row)
-            def _():
-                pltpu.make_async_remote_copy(
-                    zsend.at[r], zrecv.at[row], z_send, z_recv, device_id=(r, col), device_id_type=MESH
-                ).start()
+        zrecv[row] = zsend[row]
+
+        @pl.loop(0, rows - 1)
+        def _(i):
+            k = i // 2
+            away = half + (k + 1) // 2 * (2 * lax.rem(k, 2) - 1)
+            r = jnp.where(i < rows - 2, lax.rem(z + away, nz) * 2 + lax.rem(i, 2), partner)
+            pltpu.make_async_remote_copy(
+                zsend.at[r], zrecv.at[row], z_send, z_recv, device_id=(r, col), device_id_type=MESH
+            ).start()
 
     slots_a = list(range(zero - near, zero + near + 1))
-    slots_b = [s for s in range(nz) if s not in slots_a]
-    off = lax.rem(col - z + zero + nz, nz)
-    is_a = jnp.logical_and(off >= slots_a[0], off <= slots_a[-1])
+    slots_b = [0, nz - 2]
 
     def forward(s, h):
         if h >= 1:
             for way in range(2):
                 ring(s, h - 1, way).wait_recv()
                 ring(s, h, way).start()
-        elif s:
+        else:
             if s == 1:
                 swap_a.wait_recv()
             else:
@@ -247,43 +248,37 @@
             ring(s, 0, 0).start()
             ring(s, 0, 1).start()
 
-    for t in range(1, half + LAG):
-        for s in range(3):
-            h = t if s == 0 else t - LAG
-            if h < half:
-                forward(s, h)
-        if t == 1:
-            load_f.wait()
-        if 1 <= t <= 2:
+    forward(0, 1)
+    load_f.wait()
+    for h in range(near):
+        forward(1, h)
+        forward(2, h)
+        forward(0, h + 2)
+        if h < 2:
             for i in range(2):
-                split_f(fown, yh * sites, 2 * t - 2 + i)
-        if t == 2:
+                split_f(fown, yh * sites, 2 * h + i)
+        if h == min(2, near - 1):
             swap_p.wait_recv()
             build_onehot()
-        if 3 <= t <= 6 and half == 8:
-            swap_f[t - 3].wait_recv()
-            split_f(frecv, (1 - yh) * sites, t - 3)
-        if half != 8 and t == 1:
-            for i in range(4):
+        for i in range(4):
+            if h == max(near - 4 + i, 0):
                 swap_f[i].wait_recv()
                 split_f(frecv, (1 - yh) * sites, i)
-
-    matmul(slots_a, 0, 4, True)
-    send_partials(slots_a)
-
-    @pl.when(is_a)
-    def _():
-        finish_sites()
-
+    forward(1, near)
+    forward(2, near)
+    matmul(slots_a, 4, 0, 4)
+    send_partials(slots_a[: near // 2])
+    forward(1, near + 1)
+    send_partials(slots_a[near // 2 :], near // 2)
+    forward(2, near + 1)
+    matmul(slots_b, 2, 0, 2)
+    send_partials(slots_b)
     for s in range(3):
         for way in range(2):
             ring(s, half - 1, way).wait_recv()
-    matmul(slots_b, 0, 4, True)
-    send_partials(slots_b)
-
-    @pl.when(jnp.logical_not(is_a))
-    def _():
-        finish_sites()
+    matmul([nz - 1], 2, 0, 2)
+    send_partials([nz - 1])
+    finish_sites()
 
     swap_a.wait_send()
     swap_b.wait_send()
@@ -321,9 +316,11 @@
     return pl.pallas_call(
         functools.partial(kernel, nz, nc, kh, plants),
         out_shape=jax.ShapeDtypeStruct((24, 64), f32),
-        in_specs=[hbm, hbm] + [vmem] * 5,
+        in_specs=[hbm] * 7,
         out_specs=vmem,
         scratch_shapes=[
+            pltpu.VMEM((3, 128), f32),
+            pltpu.VMEM((2, 128), jnp.int32),
             pltpu.VMEM((12, k), f32),
             pltpu.VMEM((nz, 3, 8, kh), f32),
             pltpu.VMEM((8, kh // 2), f32),
@@ -333,18 +330,18 @@
             pltpu.VMEM((2 * sites, kh), bf16),
             pltpu.VMEM((2 * sites, kh), bf16),
             pltpu.VMEM((2, 8, 128), f32),
-            pltpu.VMEM((nz, 2 * sites, 128), bf16),
+            pltpu.VMEM((2 * sites, plants), bf16),
             pltpu.VMEM((24 * (nz - 3), 2 * sites), f32),
             pltpu.VMEM((2 * nc, 8, 384), f32),
             pltpu.VMEM((2 * nc, 8, 384), f32),
             pltpu.VMEM((rows, 8, 128), f32),
             pltpu.VMEM((rows, 8, 128), f32),
-            dma((3,)), dma((3,)), dma((3,)), dma((4,)), dma((4,)),
+            dma((8,)), dma((3,)), dma((3,)), dma((4,)), dma((4,)),
             dma((6 * half,)), dma((6 * half,)),
             dma, dma, dma, dma,
         ],
         compiler_params=pltpu.CompilerParams(
-            collective_id=0, has_side_effects=True, vmem_limit_bytes=48 * 1024 * 1024
+            collective_id=0, has_side_effects=True, vmem_limit_bytes=58 * 1024 * 1024
         ),
         cost_estimate=pl.CostEstimate(flops=3 * 2 * 24 * nz * 2 * sites * kh, bytes_accessed=4 * sites * k, transcendentals=0),
         name="band_to_plants",

time: 119 us -> 101 us (0.85)
  Pallas kernels: 112 us -> 99.4 us
  local copies, waits for them, and re-layouts: 7.1 us -> 1.31 us
    pallas_call x1, Pallas kernels: 112 us -> 99.4 us  [body(): pl.pallas_call(functools.partial(kernel, nz, nc, kh, plants), out_shape=j...]
    unnamed x15 -> x1, local copies, waits for them, and re-layouts: 7.1 us -> 1.31 us
where the time goes in v2:
time: 101 us
  Pallas kernels  99.4 us (98%)
  local copies, waits for them, and re-layouts  1.31 us (1%)
    pallas_call x1, Pallas kernels, body(): pl.pallas_call(functools.partial(kernel, nz, nc, kh, plants), out_shape=j...  99.4 us

profile of v2, /device:TPU:1, one launch (start us, length us, event | category | flops | bytes accessed | tf_op | source)
XLA Modules:
  0.0 100.7 jit_solution(5746533664753479786)
XLA Ops:
  0.0 99.4 %band_to_plants.1 = f32[24,64]{1,0:T(8,128)} custom-call(f32[128,8192]{1,0:T(8,128)} %f_ref.1, f32[12,8192]{1,0:T(8,128)} %bitcast.1, f32[128]{0:T(128)} %mean_ref.1, f32[128]{0:T(128)} %spread_ref.1, f32[128]{0:T(128)} %cap_ref.1, s32[128]{0:T(128)} %kind_ref.1, s32[128]{0:T(128)} %plant_ref.1), custom_call_target="tpu_custom_call" | custom-call | flops 2415919104 | bytes 4194304 | tf_op jit(solution)/shard_map/band_to_plants/pallas_call | solution.py:316
  99.4 1.3 %copy.9 = f32[24,64]{1,0:T(8,128)} copy(f32[24,64]{1,0:T(8,128)} %band_to_plants.1) | data formatting | bytes 12288

commit v3 on v2

--- a/solution.py
+++ b/solution.py
@@ -23,7 +23,7 @@
     nz, nc, kh, plants,
     f_ref, n_ref, mean_ref, spread_ref, cap_ref, kind_ref, plant_ref, out_ref,
     sitef, sitei, nown, nbuf, bsend, brecv, fown, frecv, fh, fl, par, onehot, acc, rsend, rrecv, zsend, zrecv,
-    loc_sem, nx_send, nx_recv, fx_send, fx_recv, ring_send, ring_recv, r_send, r_recv, z_send, z_recv,
+    loc_sem, nx_send, nx_recv, fx_send, fx_recv, ring_send, ring_recv, r_send, r_recv, z_send, z_recv, plane_sem, twin_sem,
 ):
     half = nz // 2
     zero = half - 1
@@ -43,13 +43,22 @@
     for r in (right, left):
         pl.semaphore_signal(barrier, inc=1, device_id=(r, col), device_id_type=MESH)
 
-    @pl.loop(0, peers)
-    def _(i):
-        r, c = z * 2 + i // nc, lax.rem(i, nc)
-
-        @pl.when(jnp.logical_or(r != row, c != col))
-        def _():
-            pl.semaphore_signal(barrier, inc=1, device_id=(r, c), device_id_type=MESH)
+    core, yl, x = lax.rem(col, 2), lax.rem(col // 2, 2), col // 4
+    nx = nc // 4
+    group = [(row, lax.rem(x + i, nx) * 4 + yl * 2 + core) for i in range(1, nx)]
+    flipped = col + 2 - 4 * yl
+    group += [(partner, col), (row, flipped), (partner, flipped)]
+    twin = (row, col + 1 - 2 * core)
+
+    def signal(sem, who):
+        pl.semaphore_signal(sem, inc=1, device_id=who, device_id_type=MESH)
+
+    for who in group:
+        signal(barrier, who)
+
+    @pl.when(core == 0)
+    def _():
+        signal(barrier, twin)
 
     load_a = pltpu.make_async_copy(n_ref.at[pl.ds(0, 8), pl.ds(mine, kh)], nbuf.at[zero, ua], loc_sem.at[0])
     load_n = pltpu.make_async_copy(n_ref, nown, loc_sem.at[1])
@@ -63,6 +72,43 @@
         c.start()
     load_f.start()
 
+    def to_partner(src, dst, i):
+        return pltpu.make_async_remote_copy(
+            src, dst, nx_send.at[i], nx_recv.at[i], device_id=(partner, col), device_id_type=MESH
+        )
+
+    q = kh // 2
+
+    def ring(s, h, way):
+        unit = (ua, ua, up, 1)[s]
+        slot = zero - h if way == 0 else zero + h
+        to = slot - 1 if way == 0 else slot + 1
+        if s < 2:
+            part = pl.ds(s * q, q)
+        else:
+            part = pl.ds(0, kh) if h < half - 1 else pl.ds(way * q, q)
+        if h == half - 1:
+            to = nz - 1
+        src = nbuf.at[slot, unit, :, part]
+        if s < 2 and h == 0:
+            src = n_ref.at[pl.ds(0, 8), pl.ds(pl.multiple_of(mine + s * q, q), q)]
+        i = (s * half + h) * 2 + way
+        return pltpu.make_async_remote_copy(
+            src, nbuf.at[to, unit, :, part], ring_send.at[i], ring_recv.at[i],
+            device_id=(right if way == 0 else left, col), device_id_type=MESH,
+        )
+
+    def steps(s, h):
+        return (s,) if s < 2 and h == half - 1 else (0, 1)
+
+    pl.semaphore_wait(barrier, 2 + len(group) + core)
+    for s in range(2):
+        for way in range(2):
+            ring(s, 0, way).start()
+
+    swap_a = to_partner(n_ref.at[pl.ds(0, 8), pl.ds(other, kh)], nbuf.at[zero, ua], 0)
+    swap_a.start()
+
     row_of = lax.broadcasted_iota(jnp.int32, (8, 128), 0)
     packed = jnp.zeros((8, 128), jnp.float32)
     for c in load_s:
@@ -72,40 +118,10 @@
         packed = jnp.where(row_of == i, v, packed)
     par[yh] = packed
     load_n.wait()
-    q = kh // 2
     bsend[0:4, :] = nown[8:12, pl.ds(other, q)]
     bsend[4:8, :] = nown[8:12, pl.ds(pl.multiple_of(other + q, q), q)]
-    load_a.wait()
-
-    pl.semaphore_wait(barrier, peers - 1 + 2)
-
-    def to_partner(src, dst, i):
-        return pltpu.make_async_remote_copy(
-            src, dst, nx_send.at[i], nx_recv.at[i], device_id=(partner, col), device_id_type=MESH
-        )
-
-    def ring(s, h, way):
-        unit = (ua, up, 1)[s]
-        slot = zero - h if way == 0 else zero + h
-        to = slot - 1 if way == 0 else slot + 1
-        if h < half - 1:
-            src, dst = nbuf.at[slot, unit], nbuf.at[to, unit]
-        else:
-            to = nz - 1
-            part = pl.ds(0, q) if way == 0 else pl.ds(q, q)
-            src, dst = nbuf.at[slot, unit, :, part], nbuf.at[to, unit, :, part]
-        i = (s * half + h) * 2 + way
-        return pltpu.make_async_remote_copy(
-            src, dst, ring_send.at[i], ring_recv.at[i],
-            device_id=(right if way == 0 else left, col), device_id_type=MESH,
-        )
-
-    swap_a = to_partner(n_ref.at[pl.ds(0, 8), pl.ds(other, kh)], nbuf.at[zero, ua], 0)
     swap_b = to_partner(bsend, brecv, 1)
     swap_p = to_partner(par.at[yh], par.at[yh], 2)
-    ring(0, 0, 0).start()
-    ring(0, 0, 1).start()
-    swap_a.start()
     swap_b.start()
     swap_p.start()
     swap_f = [
@@ -199,7 +215,8 @@
         for i in range(1, peers):
             tot = tot + rrecv[i]
         b = jnp.concatenate([tot[0:4, 256:384], tot[4:8, 256:384]], axis=1)
-        samples = jnp.concatenate([tot[:, 0:256], b, b], axis=0)
+        a = tot[:, 0:256]
+        samples = jnp.concatenate([a, a[6:8], b, b[0:2]], axis=0)
         p = jnp.concatenate([par[0], par[1]], axis=1)
         speed = p[0:1] + p[1:2] * samples
         positive = jnp.maximum(speed, 0.0)
@@ -219,7 +236,7 @@
             a, c = sums[0:8, 128 * j : 128 * (j + 1)], sums[8:16, 128 * j : 128 * (j + 1)]
             msgs = jnp.where(low, a, pltpu.roll(c, 64, 1)), jnp.where(low, pltpu.roll(a, 64, 1), c)
             for y in range(2):
-                zsend[2 * j + y] = msgs[y]
+                zsend[2 * j + y] = msgs[y][0:6]
 
         zrecv[row] = zsend[row]
 
@@ -236,24 +253,34 @@
     slots_b = [0, nz - 2]
 
     def forward(s, h):
-        if h >= 1:
-            for way in range(2):
+        if h == 0 and s == 2:
+            swap_a.wait_recv()
+        if h == 0 and s == 3:
+            build_t1()
+        for way in range(2):
+            if h:
                 ring(s, h - 1, way).wait_recv()
+            if way in steps(s, h):
                 ring(s, h, way).start()
-        else:
-            if s == 1:
-                swap_a.wait_recv()
-            else:
-                build_t1()
-            ring(s, 0, 0).start()
-            ring(s, 0, 1).start()
+
+    for who in group:
+        signal(plane_sem, who)
+
+    @pl.when(core == 1)
+    def _():
+        signal(plane_sem, twin)
 
     forward(0, 1)
+    forward(1, 1)
     load_f.wait()
+    load_a.wait()
+    pl.semaphore_wait(plane_sem, len(group) + 1 - core)
+    signal(twin_sem, twin)
     for h in range(near):
-        forward(1, h)
         forward(2, h)
+        forward(3, h)
         forward(0, h + 2)
+        forward(1, h + 2)
         if h < 2:
             for i in range(2):
                 split_f(fown, yh * sites, 2 * h + i)
@@ -264,17 +291,18 @@
             if h == max(near - 4 + i, 0):
                 swap_f[i].wait_recv()
                 split_f(frecv, (1 - yh) * sites, i)
-    forward(1, near)
     forward(2, near)
-    matmul(slots_a, 4, 0, 4)
+    forward(3, near)
+    pl.semaphore_wait(twin_sem, 1)
+    matmul(slots_a, 2, 0, 2)
     send_partials(slots_a[: near // 2])
-    forward(1, near + 1)
+    forward(2, near + 1)
     send_partials(slots_a[near // 2 :], near // 2)
-    forward(2, near + 1)
-    matmul(slots_b, 2, 0, 2)
+    forward(3, near + 1)
+    matmul(slots_b, 1, 0, 1)
     send_partials(slots_b)
-    for s in range(3):
-        for way in range(2):
+    for s in range(4):
+        for way in steps(s, half - 1):
             ring(s, half - 1, way).wait_recv()
     matmul([nz - 1], 2, 0, 2)
     send_partials([nz - 1])
@@ -285,9 +313,9 @@
     swap_p.wait_send()
     for c in swap_f:
         c.wait_send()
-    for s in range(3):
+    for s in range(4):
         for h in range(half):
-            for way in range(2):
+            for way in steps(s, h):
                 ring(s, h, way).wait_send()
     pltpu.make_async_copy(rsend.at[pl.ds(0, peers - 1)], rsend.at[pl.ds(0, peers - 1)], r_send).wait()
     pltpu.make_async_copy(zsend.at[pl.ds(0, rows - 1)], zsend.at[pl.ds(0, rows - 1)], z_send).wait()
@@ -296,10 +324,7 @@
     for i in range(1, nz):
         s0 = s0 + zrecv[2 * i]
         s1 = s1 + zrecv[2 * i + 1]
-    out_ref[0:8, :] = s0[:, 0:64]
-    out_ref[8:12, :] = s0[0:4, 64:128]
-    out_ref[12:20, :] = s1[:, 0:64]
-    out_ref[20:24, :] = s1[0:4, 64:128]
+    out_ref[...] = jnp.concatenate([s0[:, 0:64], s0[:, 64:128], s1[:, 0:64], s1[:, 64:128]], axis=0)
 
 
 def body(factor_band, normals, site_mean, site_spread, site_capacity, site_kind, site_plant):
@@ -334,11 +359,12 @@
             pltpu.VMEM((24 * (nz - 3), 2 * sites), f32),
             pltpu.VMEM((2 * nc, 8, 384), f32),
             pltpu.VMEM((2 * nc, 8, 384), f32),
-            pltpu.VMEM((rows, 8, 128), f32),
-            pltpu.VMEM((rows, 8, 128), f32),
+            pltpu.VMEM((rows, 6, 128), f32),
+            pltpu.VMEM((rows, 6, 128), f32),
             dma((8,)), dma((3,)), dma((3,)), dma((4,)), dma((4,)),
-            dma((6 * half,)), dma((6 * half,)),
+            dma((8 * half,)), dma((8 * half,)),
             dma, dma, dma, dma,
+            pltpu.SemaphoreType.REGULAR, pltpu.SemaphoreType.REGULAR,
         ],
         compiler_params=pltpu.CompilerParams(
             collective_id=0, has_side_effects=True, vmem_limit_bytes=58 * 1024 * 1024

time: 101 us -> 98.7 us (0.977)
  Pallas kernels: 99.4 us -> 97.2 us
    pallas_call x1, Pallas kernels: 99.4 us -> 97.2 us  [body(): pl.pallas_call(functools.partial(kernel, nz, nc, kh, plants), out_shape=j...]
where the time goes in v3:
time: 98.7 us; the launch traced here: 98.5 us
  Pallas kernels  97.2 us (98%)
  local copies, waits for them, and re-layouts  1.31 us (1%)
    pallas_call x1, Pallas kernels, body(): pl.pallas_call(functools.partial(kernel, nz, nc, kh, plants), out_shape=j...  97.2 us

profile of v3, /device:TPU:1, one launch (start us, length us, event | category | flops | bytes accessed | tf_op | source)
XLA Modules:
  0.0 98.5 jit_solution(10596097566308455158)
XLA Ops:
  0.0 97.2 %band_to_plants.1 = f32[24,64]{1,0:T(8,128)} custom-call(f32[128,8192]{1,0:T(8,128)} %f_ref.1, f32[12,8192]{1,0:T(8,128)} %bitcast.1, f32[128]{0:T(128)} %mean_ref.1, f32[128]{0:T(128)} %spread_ref.1, f32[128]{0:T(128)} %cap_ref.1, s32[128]{0:T(128)} %kind_ref.1, s32[128]{0:T(128)} %plant_ref.1), custom_call_target="tpu_custom_call" | custom-call | flops 2415919104 | bytes 4194304 | tf_op jit(solution)/shard_map/band_to_plants/pallas_call | solution.py:341
  97.2 1.3 %copy.9 = f32[24,64]{1,0:T(8,128)} copy(f32[24,64]{1,0:T(8,128)} %band_to_plants.1) | data formatting | bytes 12288

commit v4 on v3

--- a/solution.py
+++ b/solution.py
@@ -336,11 +336,11 @@
     plants = 64 * rows
     f32, bf16 = jnp.float32, jnp.bfloat16
     vmem = pl.BlockSpec(memory_space=pltpu.VMEM)
-    hbm = pl.BlockSpec(memory_space=pl.ANY)
+    hbm = pl.BlockSpec(memory_space=pltpu.HBM)
     dma = pltpu.SemaphoreType.DMA
     return pl.pallas_call(
         functools.partial(kernel, nz, nc, kh, plants),
-        out_shape=jax.ShapeDtypeStruct((24, 64), f32),
+        out_shape=pltpu.VMEM((24, 64), f32),
         in_specs=[hbm] * 7,
         out_specs=vmem,
         scratch_shapes=[
@@ -367,11 +367,11 @@
             pltpu.SemaphoreType.REGULAR, pltpu.SemaphoreType.REGULAR,
         ],
         compiler_params=pltpu.CompilerParams(
-            collective_id=0, has_side_effects=True, vmem_limit_bytes=58 * 1024 * 1024
+            collective_id=0, has_side_effects=True, vmem_limit_bytes=48 * 1024 * 1024
         ),
         cost_estimate=pl.CostEstimate(flops=3 * 2 * 24 * nz * 2 * sites * kh, bytes_accessed=4 * sites * k, transcendentals=0),
         name="band_to_plants",
-    )(factor_band, normals.T, site_mean, site_spread, site_capacity, site_kind, site_plant)
+    )(*(pltpu.with_memory_space_constraint(v, pltpu.HBM) for v in (factor_band, normals.T, site_mean, site_spread, site_capacity, site_kind, site_plant)))
 
 
 def solution(mesh):

time: 98.7 us -> 97.3 us (0.986)
  no operation moved by 1% of the time
where the time goes in v4:
time: 97.3 us; the launch traced here: 97.2 us
  Pallas kernels  96.6 us (99%)
    pallas_call x1, Pallas kernels, body(): pl.pallas_call(functools.partial(kernel, nz, nc, kh, plants), out_shape=p...  96.6 us

profile of v4, /device:TPU:1, one launch (start us, length us, event | category | flops | bytes accessed | tf_op | source)
XLA Modules:
  0.0 97.2 jit_solution(9689068138026433043)
XLA Ops:
  0.0 96.6 %band_to_plants.1 = f32[24,64]{1,0:T(8,128)S(1)} custom-call(f32[128,8192]{1,0:T(8,128)} %f_ref.1, f32[12,8192]{1,0:T(8,128)} %bitcast.1, f32[128]{0:T(128)} %mean_ref.1, f32[128]{0:T(128)} %spread_ref.1, f32[128]{0:T(128)} %cap_ref.1, s32[128]{0:T(128)} %kind_ref.1, s32[128]{0:T(128)} %plant_ref.1), custom_call_target="tpu_custom_call" | custom-call | flops 2415919104 | bytes 4194304 | tf_op jit(solution)/shard_map/band_to_plants/pallas_call | solution.py:341
  96.6 0.6 copy.9

commit v5 on v4

--- a/solution.py
+++ b/solution.py
@@ -164,14 +164,15 @@
             lane = lax.broadcasted_iota(jnp.int32, (2 * sites, 128), 1) + j * 128
             onehot[:, pl.ds(pl.multiple_of(j * 128, 128), 128)] = jnp.where(ids == lane.astype(jnp.float32), 1.0, 0.0).astype(jnp.bfloat16)
 
-    def matmul(slots, parts, k_from, k_to):
+    def matmul(slots, parts, k_from, k_to, units=()):
         step = kh // parts
-        m = 24 * len(slots)
+        m = 24 * len(slots) + 8 * len(units)
 
         @pl.loop(k_from, k_to)
         def _(k):
             cols = pl.ds(pl.multiple_of(k * step, step), step)
-            x = jnp.concatenate([nbuf[s, :, :, cols].reshape(24, step) for s in slots], axis=0)
+            x = [nbuf[s, :, :, cols].reshape(24, step) for s in slots]
+            x = jnp.concatenate(x + [nbuf[nz - 1, u, :, cols] for u in units], axis=0)
             hi = x.astype(jnp.bfloat16).astype(jnp.float32)
             hl = jnp.concatenate([hi, x - hi], axis=0).astype(jnp.bfloat16)
             t = nt_dot(hl, fh[:, cols])
@@ -208,6 +209,23 @@
                         rsend.at[2 * s + y], rrecv.at[me], r_send, r_recv,
                         device_id=(z * 2 + y, block), device_id_type=MESH,
                     ).start()
+
+    def send_last(y, msg, lanes):
+        me, block = yh * nc + col, lax.rem(z + half, nz)
+        self_ = jnp.logical_and(block == col, yh == y)
+
+        @pl.when(self_)
+        def _():
+            rrecv[me, :, lanes] = msg
+
+        @pl.when(jnp.logical_not(self_))
+        def _():
+            i = 2 * (nz - 1) + y
+            rsend[i, :, lanes] = msg
+            pltpu.make_async_remote_copy(
+                rsend.at[i, :, lanes], rrecv.at[me, :, lanes], r_send, r_recv,
+                device_id=(z * 2 + y, block), device_id_type=MESH,
+            ).start()
 
     def finish_sites():
         pltpu.make_async_copy(rrecv.at[pl.ds(0, peers - 1)], rrecv.at[pl.ds(0, peers - 1)], r_recv).wait()
@@ -299,13 +317,19 @@
     forward(2, near + 1)
     send_partials(slots_a[near // 2 :], near // 2)
     forward(3, near + 1)
-    matmul(slots_b, 1, 0, 1)
-    send_partials(slots_b)
-    for s in range(4):
+    for s in range(3):
         for way in steps(s, half - 1):
             ring(s, half - 1, way).wait_recv()
-    matmul([nz - 1], 2, 0, 2)
-    send_partials([nz - 1])
+    matmul(slots_b, 1, 0, 1, (0, 2))
+    for y in range(2):
+        send_last(y, acc[48 + 8 * y : 56 + 8 * y, :], pl.ds(0, 256))
+    send_partials(slots_b)
+    for way in range(2):
+        ring(3, half - 1, way).wait_recv()
+    matmul([], 2, 0, 2, (1,))
+    for y in range(2):
+        b = acc[4 * y : 4 * y + 4, :]
+        send_last(y, jnp.concatenate([b[:, 0:128], b[:, 128:256]], axis=0), pl.ds(256, 128))
     finish_sites()
 
     swap_a.wait_send()

time: 97.3 us -> 97 us (level)
  no operation moved by 1% of the time
where the time goes in v5:
time: 97 us; the launch traced here: 96.9 us
  Pallas kernels  96.3 us (99%)
    pallas_call x1, Pallas kernels, body(): pl.pallas_call(functools.partial(kernel, nz, nc, kh, plants), out_shape=p...  96.3 us

profile of v5, /device:TPU:1, one launch (start us, length us, event | category | flops | bytes accessed | tf_op | source)
XLA Modules:
  0.0 96.9 jit_solution(15028312475927614603)
XLA Ops:
  0.0 96.3 %band_to_plants.1 = f32[24,64]{1,0:T(8,128)S(1)} custom-call(f32[128,8192]{1,0:T(8,128)} %f_ref.1, f32[12,8192]{1,0:T(8,128)} %bitcast.1, f32[128]{0:T(128)} %mean_ref.1, f32[128]{0:T(128)} %spread_ref.1, f32[128]{0:T(128)} %cap_ref.1, s32[128]{0:T(128)} %kind_ref.1, s32[128]{0:T(128)} %plant_ref.1), custom_call_target="tpu_custom_call" | custom-call | flops 2415919104 | bytes 4194304 | tf_op jit(solution)/shard_map/band_to_plants/pallas_call | solution.py:365
  96.3 0.6 copy.9

commit v6 on v5

--- a/solution.py
+++ b/solution.py
@@ -326,7 +326,7 @@
     send_partials(slots_b)
     for way in range(2):
         ring(3, half - 1, way).wait_recv()
-    matmul([], 2, 0, 2, (1,))
+        matmul([], 2, way, way + 1, (1,))
     for y in range(2):
         b = acc[4 * y : 4 * y + 4, :]
         send_last(y, jnp.concatenate([b[:, 0:128], b[:, 128:256]], axis=0), pl.ds(256, 128))

time: 97 us -> 98.4 us (1.014)
  Pallas kernels: 96.3 us -> 97.7 us
    pallas_call x1, Pallas kernels: 96.3 us -> 97.7 us  [body(): pl.pallas_call(functools.partial(kernel, nz, nc, kh, plants), out_shape=p...]
where the time goes in v6:
time: 98.4 us; the launch traced here: 98.3 us
  Pallas kernels  97.7 us (99%)
    pallas_call x1, Pallas kernels, body(): pl.pallas_call(functools.partial(kernel, nz, nc, kh, plants), out_shape=p...  97.7 us

profile of v6, /device:TPU:1, one launch (start us, length us, event | category | flops | bytes accessed | tf_op | source)
XLA Modules:
  0.0 98.3 jit_solution(15950315041073239745)
XLA Ops:
  0.0 97.7 %band_to_plants.1 = f32[24,64]{1,0:T(8,128)S(1)} custom-call(f32[128,8192]{1,0:T(8,128)} %f_ref.1, f32[12,8192]{1,0:T(8,128)} %bitcast.1, f32[128]{0:T(128)} %mean_ref.1, f32[128]{0:T(128)} %spread_ref.1, f32[128]{0:T(128)} %cap_ref.1, s32[128]{0:T(128)} %kind_ref.1, s32[128]{0:T(128)} %plant_ref.1), custom_call_target="tpu_custom_call" | custom-call | flops 2415919104 | bytes 4194304 | tf_op jit(solution)/shard_map/band_to_plants/pallas_call | solution.py:365
  97.7 0.6 copy.9
